TPU v7x, 32 devices: a whole 2x2x4 slice. The times are simulated.
32 devices in a mesh: pairs: 16 (over z, y, x), aux: 2 (over core).
Axes of the slice: x: 2, y: 2, z: 4, core: 2. Of those that a mesh axis runs over, the one named last changes fastest.
Arguments:
- amplitudes: bfloat16 [256, 128, 128], P('pairs'), may hold values from -6 to 6
- pno_coef: bfloat16 [256, 256, 128], P('pairs'), may hold values from -0.75 to 0.75
- ladder_ints: bfloat16 [320, 128, 128], P('aux'), may hold values from -0.3125 to 0.3125
- coulomb_ints: bfloat16 [256, 128, 128], P(('pairs', 'aux')), may hold values from -6 to 6
- pno_energy: float32 [256, 128], P(('pairs', 'aux')), may hold values from 0.3 to 3
- link_owner: int32 [3072, 1], P(('pairs', 'aux')), may hold values from 0 to 15; in each aligned block of 96 rows (0 to 95, 96 to 191, ...) at most 8 rows name the same one
- link_local: int32 [3072, 1], P(('pairs', 'aux')), may hold values from 0 to 15
Outputs:
- updated: float32 [256, 128, 128], P(('pairs', 'aux'))
Inputs may be any that keep to these rules, and one draw needn't show every extreme that they name: `link_owner`: in each device's aligned block of 96 rows no owner group is named by more than 8 rows, a bound that some block reaches.
All inputs are finite; a program needn't handle non-finite values.
Results may differ from a plain program's by a relative error of at most 0.0033.
Values may be sent and summed in bfloat16 or wider, within the bound.
A program may use at most 128 MiB of HBM per device.

v0:
```python
import jax
import jax.numpy as jnp
from jax import lax
from jax.sharding import PartitionSpec as P


def local(amplitudes, pno_coef, ladder_ints, coulomb_ints, pno_energy, link_owner, link_local):
    groups = lax.axis_size("pairs")
    pair_dev = amplitudes.shape[0]
    own_rows = coulomb_ints.shape[0]
    slot_count = link_owner.shape[0]
    per_slice = slot_count // pair_dev
    capacity = max(2, (5 * slot_count + 4 * groups - 1) // (4 * groups))
    pno_width = amplitudes.shape[1]
    pao_width = pno_coef.shape[1]
    owner_group = link_owner[:, 0]
    local_index = link_local[:, 0]
    slot_order = jnp.arange(slot_count, dtype=jnp.int32)
    same_owner = (owner_group[:, None] == owner_group[None, :]) & (
        slot_order[None, :] < slot_order[:, None]
    )
    slot_rank = jnp.sum(same_owner.astype(jnp.int32), axis=1)
    bucket = owner_group * capacity + slot_rank
    places = jnp.arange(groups * capacity, dtype=jnp.int32)
    match_table = (bucket[:, None] == places[None, :]).astype(jnp.int32)
    wanted = jnp.sum(match_table * (local_index[:, None] + 1), axis=0) - 1
    asked_rows = lax.all_to_all(
        wanted.reshape(groups, capacity), "pairs", split_axis=0, concat_axis=0, tiled=True
    )
    present = asked_rows >= 0
    picked = jnp.maximum(asked_rows, 0)
    nothing = jnp.zeros((), jnp.bfloat16)
    amp_items = jnp.where(present[:, :, None, None], amplitudes[picked], nothing)
    coef_items = jnp.where(present[:, :, None, None], pno_coef[picked], nothing)
    got_amp, got_coef = (
        lax.all_to_all(amp_items, "pairs", split_axis=0, concat_axis=0, tiled=True),
        lax.all_to_all(coef_items, "pairs", split_axis=0, concat_axis=0, tiled=True),
    )
    flat_amp = got_amp.reshape(groups * capacity, pno_width, pno_width)
    flat_coef = got_coef.reshape(groups * capacity, pao_width, pno_width)
    key_rows = bucket.reshape(pair_dev, per_slice)

    def pair_terms(inputs):
        coef_p, amp_p, key_row = inputs
        coef_q = flat_coef[key_row]
        amp_q = flat_amp[key_row]
        intersection = jnp.einsum(
            "ac,lad->lcd", coef_p, coef_q, preferred_element_type=jnp.float32
        ).astype(jnp.bfloat16)
        halfway = jnp.einsum(
            "lcd,lde->lce", intersection, amp_q, preferred_element_type=jnp.float32
        ).astype(jnp.bfloat16)
        total = jnp.einsum("lce,lfe->cf", halfway, intersection, preferred_element_type=jnp.float32)
        ladder_half = jnp.einsum(
            "qcd,de->qce", ladder_ints, amp_p, preferred_element_type=jnp.float32
        ).astype(jnp.bfloat16)
        total = total + jnp.einsum(
            "qce,qfe->cf", ladder_half, ladder_ints, preferred_element_type=jnp.float32
        )
        return total

    partial_value = lax.map(pair_terms, (pno_coef, amplitudes, key_rows))
    first_row = lax.axis_index("aux") * own_rows
    amp_mine = lax.dynamic_slice_in_dim(amplitudes, first_row, own_rows, 0)
    summed = lax.psum(partial_value, "aux")
    reduced = lax.dynamic_slice_in_dim(summed, first_row, own_rows, 0)
    residual = coulomb_ints.astype(jnp.float32) + reduced
    denominator = pno_energy[:, :, None] + pno_energy[:, None, :]
    return amp_mine.astype(jnp.float32) - residual / denominator


def solution(mesh):
    in_specs = (
        P("pairs", None, None),
        P("pairs", None, None),
        P("aux", None, None),
        P(("pairs", "aux"), None, None),
        P(("pairs", "aux"), None),
        P(("pairs", "aux"), None),
        P(("pairs", "aux"), None),
    )
    out_specs = P(("pairs", "aux"), None, None)
    return jax.shard_map(local, mesh=mesh, in_specs=in_specs, out_specs=out_specs, check_vma=False)
```

profile of v0, /device:TPU:0, one launch (start us, length us, event | category | flops | bytes accessed | tf_op | source)
XLA Modules:
  0.0 595.2 jit_solution(5453568657038118061)
XLA Ops:
  9.0 15.4 %all_to_all.16 = s32[16,1,8]{2,1,0:T(1,128)S(1)} all-to-all(s32[16,1,8]{2,1,0:T(1,128)S(1)} %bitcast.99), channel_id=1, replica_groups=mesh['pairs'=16,'aux'=2] {'pairs'}, dimensions={0} | all-to-all | bytes 1024 | tf_op jit(solution)/shard_map/all_to_all | solution.py:27
  38.0 6.5 %gather_fusion.2 = bf16[128,256,128]{2,1,0:T(8,128)(2,1)} fusion(bf16[16,256,128]{2,1,0:T(8,128)(2,1)S(1)} %copy-done, s32[1024]{0:T(1024)S(1)} %pad_clamp_fusion.1), kind=kCustom, calls=%fused_computation.2 | custom fusion | bytes 16777728 | tf_op jit(solution)/shard_map/gather | solution.py:34
  44.5 7.2 %broadcast_select_fusion = bf16[16,8,256,128]{3,2,1,0:T(8,128)(2,1)} fusion(bf16[16,8,256,128]{3,2,1,0:T(8,128)(2,1)} %bitcast.97, pred[16,8]{1,0:T(8,128)(4,1)S(1)} %copy.35), kind=kLoop, calls=%fused_computation.28 | loop fusion | flops 4194304 | bytes 16777344 | tf_op jit(solution)/shard_map/jit(_where)/select_n | solution.py:34
  51.8 64.8 %all-to-all-done.2 = bf16[16,8,128,128]{3,2,1,0:T(8,128)(2,1)} async-done(((bf16[16,8,128,128]{3,2,1,0:T(8,128)(2,1)}), bf16[16,8,128,128]{3,2,1,0:T(8,128)(2,1)}, u32[]{:S(2)}, u32[]{:S(2)}) %all-to-all-start.2) | async-done | bytes 4194336 | tf_op jit(solution)/shard_map/all_to_all | solution.py:36
  116.5 18.6 %all-to-all-start.1 = ((bf16[16,8,256,128]{3,2,1,0:T(8,128)(2,1)}), bf16[16,8,256,128]{3,2,1,0:T(8,128)(2,1)}, u32[]{:S(2)}, u32[]{:S(2)}) async-start(bf16[16,8,256,128]{3,2,1,0:T(8,128)(2,1)} %broadcast_select_fusion), calls=%async_computation.1 | async-start | bytes 16777216 | tf_op jit(solution)/shard_map/all_to_all | solution.py:37
  135.4 154.4 %all-to-all-done.1 = bf16[16,8,256,128]{3,2,1,0:T(8,128)(2,1)} async-done(((bf16[16,8,256,128]{3,2,1,0:T(8,128)(2,1)}), bf16[16,8,256,128]{3,2,1,0:T(8,128)(2,1)}, u32[]{:S(2)}, u32[]{:S(2)}) %all-to-all-start.1) | async-done | bytes 8388640 | tf_op jit(solution)/shard_map/all_to_all | solution.py:37
  289.8 242.8 %while.10 = (s32[]{:T(128)}, f32[16,128,128]{2,1,0:T(8,128)}, s32[16,6]{1,0:T(8,128)S(1)}, bf16[128,256,128]{2,1,0:T(8,128)(2,1)}, bf16[16,256,128]{2,1,0:T(8,12...) while((s32[]{:T(128)}, f32[16,128,128]{2,1,0:T(8,128)}, ...), condition=%wide.region_3.4_spmd, body=%wide.region_2.3_spmd.sunk | while | flops 1445676032 | bytes 12948701 | solution.py:62
  297.4 7.6 %fusion.61 = f32[16,128,128]{2,1,0:T(8,128)} fusion(f32[16,128,128]{2,1,0:T(8,128)} %get-tuple-element.141, s32[]{:T(128)} %get-tuple-element.140, f32[128,128]{1,0:T(8,128)S(1)} %fusion.60, bf16[160,128,128]{2,1,0:T(8,128)(2,1)} %get-tuple-element.156, bf16[16,128,128]{2,1,0:T(8,128)(2,1)S(1)} %get-tuple-element.155), kind=kOutput, calls=%fused_computation.14.clone.1 | convolution fusion | flops 1344815104 | bytes 10650624 | tf_op jit(solution)/shard_map/while/body/eval_jaxpr/qce,qfe->cf/dot_general | solution.py:57
  312.6 7.6 %fusion.61 = f32[16,128,128]{2,1,0:T(8,128)} fusion(f32[16,128,128]{2,1,0:T(8,128)} %get-tuple-element.141, s32[]{:T(128)} %get-tuple-element.140, f32[128,128]{1,0:T(8,128)S(1)} %fusion.60, bf16[160,128,128]{2,1,0:T(8,128)(2,1)} %get-tuple-element.156, bf16[16,128,128]{2,1,0:T(8,128)(2,1)S(1)} %get-tuple-element.155), kind=kOutput, calls=%fused_computation.14.clone.1 | convolution fusion | flops 1344815104 | bytes 10650624 | tf_op jit(solution)/shard_map/while/body/eval_jaxpr/qce,qfe->cf/dot_general | solution.py:57
  327.7 7.6 %fusion.61 = f32[16,128,128]{2,1,0:T(8,128)} fusion(f32[16,128,128]{2,1,0:T(8,128)} %get-tuple-element.141, s32[]{:T(128)} %get-tuple-element.140, f32[128,128]{1,0:T(8,128)S(1)} %fusion.60, bf16[160,128,128]{2,1,0:T(8,128)(2,1)} %get-tuple-element.156, bf16[16,128,128]{2,1,0:T(8,128)(2,1)S(1)} %get-tuple-element.155), kind=kOutput, calls=%fused_computation.14.clone.1 | convolution fusion | flops 1344815104 | bytes 10650624 | tf_op jit(solution)/shard_map/while/body/eval_jaxpr/qce,qfe->cf/dot_general | solution.py:57
  342.9 7.6 %fusion.61 = f32[16,128,128]{2,1,0:T(8,128)} fusion(f32[16,128,128]{2,1,0:T(8,128)} %get-tuple-element.141, s32[]{:T(128)} %get-tuple-element.140, f32[128,128]{1,0:T(8,128)S(1)} %fusion.60, bf16[160,128,128]{2,1,0:T(8,128)(2,1)} %get-tuple-element.156, bf16[16,128,128]{2,1,0:T(8,128)(2,1)S(1)} %get-tuple-element.155), kind=kOutput, calls=%fused_computation.14.clone.1 | convolution fusion | flops 1344815104 | bytes 10650624 | tf_op jit(solution)/shard_map/while/body/eval_jaxpr/qce,qfe->cf/dot_general | solution.py:57
  358.1 7.6 %fusion.61 = f32[16,128,128]{2,1,0:T(8,128)} fusion(f32[16,128,128]{2,1,0:T(8,128)} %get-tuple-element.141, s32[]{:T(128)} %get-tuple-element.140, f32[128,128]{1,0:T(8,128)S(1)} %fusion.60, bf16[160,128,128]{2,1,0:T(8,128)(2,1)} %get-tuple-element.156, bf16[16,128,128]{2,1,0:T(8,128)(2,1)S(1)} %get-tuple-element.155), kind=kOutput, calls=%fused_computation.14.clone.1 | convolution fusion | flops 1344815104 | bytes 10650624 | tf_op jit(solution)/shard_map/while/body/eval_jaxpr/qce,qfe->cf/dot_general | solution.py:57
  373.2 7.6 %fusion.61 = f32[16,128,128]{2,1,0:T(8,128)} fusion(f32[16,128,128]{2,1,0:T(8,128)} %get-tuple-element.141, s32[]{:T(128)} %get-tuple-element.140, f32[128,128]{1,0:T(8,128)S(1)} %fusion.60, bf16[160,128,128]{2,1,0:T(8,128)(2,1)} %get-tuple-element.156, bf16[16,128,128]{2,1,0:T(8,128)(2,1)S(1)} %get-tuple-element.155), kind=kOutput, calls=%fused_computation.14.clone.1 | convolution fusion | flops 1344815104 | bytes 10650624 | tf_op jit(solution)/shard_map/while/body/eval_jaxpr/qce,qfe->cf/dot_general | solution.py:57
  388.4 7.6 %fusion.61 = f32[16,128,128]{2,1,0:T(8,128)} fusion(f32[16,128,128]{2,1,0:T(8,128)} %get-tuple-element.141, s32[]{:T(128)} %get-tuple-element.140, f32[128,128]{1,0:T(8,128)S(1)} %fusion.60, bf16[160,128,128]{2,1,0:T(8,128)(2,1)} %get-tuple-element.156, bf16[16,128,128]{2,1,0:T(8,128)(2,1)S(1)} %get-tuple-element.155), kind=kOutput, calls=%fused_computation.14.clone.1 | convolution fusion | flops 1344815104 | bytes 10650624 | tf_op jit(solution)/shard_map/while/body/eval_jaxpr/qce,qfe->cf/dot_general | solution.py:57
  403.6 7.6 %fusion.61 = f32[16,128,128]{2,1,0:T(8,128)} fusion(f32[16,128,128]{2,1,0:T(8,128)} %get-tuple-element.141, s32[]{:T(128)} %get-tuple-element.140, f32[128,128]{1,0:T(8,128)S(1)} %fusion.60, bf16[160,128,128]{2,1,0:T(8,128)(2,1)} %get-tuple-element.156, bf16[16,128,128]{2,1,0:T(8,128)(2,1)S(1)} %get-tuple-element.155), kind=kOutput, calls=%fused_computation.14.clone.1 | convolution fusion | flops 1344815104 | bytes 10650624 | tf_op jit(solution)/shard_map/while/body/eval_jaxpr/qce,qfe->cf/dot_general | solution.py:57
  418.8 7.6 %fusion.61 = f32[16,128,128]{2,1,0:T(8,128)} fusion(f32[16,128,128]{2,1,0:T(8,128)} %get-tuple-element.141, s32[]{:T(128)} %get-tuple-element.140, f32[128,128]{1,0:T(8,128)S(1)} %fusion.60, bf16[160,128,128]{2,1,0:T(8,128)(2,1)} %get-tuple-element.156, bf16[16,128,128]{2,1,0:T(8,128)(2,1)S(1)} %get-tuple-element.155), kind=kOutput, calls=%fused_computation.14.clone.1 | convolution fusion | flops 1344815104 | bytes 10650624 | tf_op jit(solution)/shard_map/while/body/eval_jaxpr/qce,qfe->cf/dot_general | solution.py:57
  433.9 7.6 %fusion.61 = f32[16,128,128]{2,1,0:T(8,128)} fusion(f32[16,128,128]{2,1,0:T(8,128)} %get-tuple-element.141, s32[]{:T(128)} %get-tuple-element.140, f32[128,128]{1,0:T(8,128)S(1)} %fusion.60, bf16[160,128,128]{2,1,0:T(8,128)(2,1)} %get-tuple-element.156, bf16[16,128,128]{2,1,0:T(8,128)(2,1)S(1)} %get-tuple-element.155), kind=kOutput, calls=%fused_computation.14.clone.1 | convolution fusion | flops 1344815104 | bytes 10650624 | tf_op jit(solution)/shard_map/while/body/eval_jaxpr/qce,qfe->cf/dot_general | solution.py:57
  449.1 7.6 %fusion.61 = f32[16,128,128]{2,1,0:T(8,128)} fusion(f32[16,128,128]{2,1,0:T(8,128)} %get-tuple-element.141, s32[]{:T(128)} %get-tuple-element.140, f32[128,128]{1,0:T(8,128)S(1)} %fusion.60, bf16[160,128,128]{2,1,0:T(8,128)(2,1)} %get-tuple-element.156, bf16[16,128,128]{2,1,0:T(8,128)(2,1)S(1)} %get-tuple-element.155), kind=kOutput, calls=%fused_computation.14.clone.1 | convolution fusion | flops 1344815104 | bytes 10650624 | tf_op jit(solution)/shard_map/while/body/eval_jaxpr/qce,qfe->cf/dot_general | solution.py:57
  464.3 7.6 %fusion.61 = f32[16,128,128]{2,1,0:T(8,128)} fusion(f32[16,128,128]{2,1,0:T(8,128)} %get-tuple-element.141, s32[]{:T(128)} %get-tuple-element.140, f32[128,128]{1,0:T(8,128)S(1)} %fusion.60, bf16[160,128,128]{2,1,0:T(8,128)(2,1)} %get-tuple-element.156, bf16[16,128,128]{2,1,0:T(8,128)(2,1)S(1)} %get-tuple-element.155), kind=kOutput, calls=%fused_computation.14.clone.1 | convolution fusion | flops 1344815104 | bytes 10650624 | tf_op jit(solution)/shard_map/while/body/eval_jaxpr/qce,qfe->cf/dot_general | solution.py:57
  479.5 7.6 %fusion.61 = f32[16,128,128]{2,1,0:T(8,128)} fusion(f32[16,128,128]{2,1,0:T(8,128)} %get-tuple-element.141, s32[]{:T(128)} %get-tuple-element.140, f32[128,128]{1,0:T(8,128)S(1)} %fusion.60, bf16[160,128,128]{2,1,0:T(8,128)(2,1)} %get-tuple-element.156, bf16[16,128,128]{2,1,0:T(8,128)(2,1)S(1)} %get-tuple-element.155), kind=kOutput, calls=%fused_computation.14.clone.1 | convolution fusion | flops 1344815104 | bytes 10650624 | tf_op jit(solution)/shard_map/while/body/eval_jaxpr/qce,qfe->cf/dot_general | solution.py:57
  494.6 7.6 %fusion.61 = f32[16,128,128]{2,1,0:T(8,128)} fusion(f32[16,128,128]{2,1,0:T(8,128)} %get-tuple-element.141, s32[]{:T(128)} %get-tuple-element.140, f32[128,128]{1,0:T(8,128)S(1)} %fusion.60, bf16[160,128,128]{2,1,0:T(8,128)(2,1)} %get-tuple-element.156, bf16[16,128,128]{2,1,0:T(8,128)(2,1)S(1)} %get-tuple-element.155), kind=kOutput, calls=%fused_computation.14.clone.1 | convolution fusion | flops 1344815104 | bytes 10650624 | tf_op jit(solution)/shard_map/while/body/eval_jaxpr/qce,qfe->cf/dot_general | solution.py:57
  509.8 7.6 %fusion.61 = f32[16,128,128]{2,1,0:T(8,128)} fusion(f32[16,128,128]{2,1,0:T(8,128)} %get-tuple-element.141, s32[]{:T(128)} %get-tuple-element.140, f32[128,128]{1,0:T(8,128)S(1)} %fusion.60, bf16[160,128,128]{2,1,0:T(8,128)(2,1)} %get-tuple-element.156, bf16[16,128,128]{2,1,0:T(8,128)(2,1)S(1)} %get-tuple-element.155), kind=kOutput, calls=%fused_computation.14.clone.1 | convolution fusion | flops 1344815104 | bytes 10650624 | tf_op jit(solution)/shard_map/while/body/eval_jaxpr/qce,qfe->cf/dot_general | solution.py:57
  525.0 7.6 %fusion.61 = f32[16,128,128]{2,1,0:T(8,128)} fusion(f32[16,128,128]{2,1,0:T(8,128)} %get-tuple-element.141, s32[]{:T(128)} %get-tuple-element.140, f32[128,128]{1,0:T(8,128)S(1)} %fusion.60, bf16[160,128,128]{2,1,0:T(8,128)(2,1)} %get-tuple-element.156, bf16[16,128,128]{2,1,0:T(8,128)(2,1)S(1)} %get-tuple-element.155), kind=kOutput, calls=%fused_computation.14.clone.1 | convolution fusion | flops 1344815104 | bytes 10650624 | tf_op jit(solution)/shard_map/while/body/eval_jaxpr/qce,qfe->cf/dot_general | solution.py:57
  532.6 53.7 %all-reduce.2.cloned.1.call-done = f32[16,128,128]{2,1,0:T(8,128)} async-done(((f32[16,128,128]{2,1,0:T(8,128)}), f32[16,128,128]{2,1,0:T(8,128)}) %all-reduce.2.cloned.1.call-update) | async-done | bytes 1048592 | tf_op jit(solution)/shard_map/psum | solution.py:65
  (127 shorter events, 138.5 us)
Async XLA Ops:
  33.3 4.7 copy-start
  33.3 83.2 %all-to-all-start.2 = ((bf16[16,8,128,128]{3,2,1,0:T(8,128)(2,1)}), bf16[16,8,128,128]{3,2,1,0:T(8,128)(2,1)}, u32[]{:S(2)}, u32[]{:S(2)}) async-start(bf16[16,8,128,128]{3,2,1,0:T(8,128)(2,1)} %broadcast_select_fusion.1), calls=%async_computation.2 | async-start | bytes 8388608 | tf_op jit(solution)/shard_map/all_to_all | solution.py:36
  51.7 238.0 %copy-start.1 = (bf16[16,128,128]{2,1,0:T(8,128)(2,1)S(1)}, bf16[16,128,128]{2,1,0:T(8,128)(2,1)}, u32[]{:S(2)}) copy-start(bf16[16,128,128]{2,1,0:T(8,128)(2,1)} %param.9) | copy-start | bytes 1572868
  116.5 173.3 %all-to-all-start.1 = ((bf16[16,8,256,128]{3,2,1,0:T(8,128)(2,1)}), bf16[16,8,256,128]{3,2,1,0:T(8,128)(2,1)}, u32[]{:S(2)}, u32[]{:S(2)}) async-start(bf16[16,8,256,128]{3,2,1,0:T(8,128)(2,1)} %broadcast_select_fusion), calls=%async_computation.1 | async-start | bytes 16777216 | tf_op jit(solution)/shard_map/all_to_all | solution.py:37
  135.1 451.2 %all-reduce.2.cloned.1.call-start = ((), (), s32[]{:S(2)}) async-start(), calls=%async_computation.3 | async-start | bytes 2097152 | tf_op jit(solution)/shard_map/psum | solution.py:65
  289.8 296.5 %copy-start.2 = (bf16[8,128,128]{2,1,0:T(8,128)(2,1)S(1)}, bf16[8,128,128]{2,1,0:T(8,128)(2,1)}, u32[]{:S(2)}) copy-start(bf16[8,128,128]{2,1,0:T(8,128)(2,1)} %param.12) | copy-start | bytes 786436
  289.8 296.5 %copy-start.3 = (f32[8,128]{1,0:T(8,128)S(1)}, f32[8,128]{1,0:T(8,128)}, u32[]{:S(2)}) copy-start(f32[8,128]{1,0:T(8,128)} %param.13) | copy-start | bytes 12292
Sparse Core Ops, SparseCore 0:
  532.7 53.5 all-reduce.1
where the time goes:
time: 597 us; the launch traced here: 595 us
  waiting for transfers between devices  273 us (46%)
  matrix products  134 us (22%)
  local copies, waits for them, and re-layouts  120 us (20%)
  starting transfers between devices  23.3 us (4%)
  other arithmetic  16.4 us (3%)
  blocking collectives  15.4 us (3%)
  between operations  13.5 us (2%)
    all_to_all x1, waiting for transfers between devices, local(): lax.all_to_all(coef_items, 'pairs', split_axis=0, concat_axis=0, tiled=True)  154 us
    dot_general x16, matrix products, pair_terms(): jnp.einsum('qce,qfe->cf', ladder_half, ladder_ints, preferred_element_typ...  122 us
    all_to_all x1, waiting for transfers between devices, local(): lax.all_to_all(amp_items, 'pairs', split_axis=0, concat_axis=0, tiled=True)  64.8 us
    gather x16, local copies, waits for them, and re-layouts, pair_terms(): coef_q = flat_coef[key_row]  64.1 us
    psum x1, waiting for transfers between devices, local(): summed = lax.psum(partial_value, 'aux')  53.7 us
    gather x16, local copies, waits for them, and re-layouts, pair_terms(): amp_q = flat_amp[key_row]  44.3 us
    all_to_all x1, starting transfers between devices, local(): lax.all_to_all(coef_items, 'pairs', split_axis=0, concat_axis=0, tiled=True)  18.6 us
    all_to_all x1, blocking collectives, local(): lax.all_to_all(wanted.reshape(groups, capacity), 'pairs', split_axis=0, c...  15.4 us
  transfers between devices with their start and end apart: 3, of which 3 were waited for; matrix products, arithmetic and copies ran while one was open for 2% of the time, Pallas kernels for 0%

commit v1 on v0

v1 whole, which is shorter than its diff:
```python
import functools

import jax
import jax.numpy as jnp
from jax import lax
from jax.experimental import pallas as pl
from jax.experimental.pallas import tpu as pltpu
from jax.sharding import PartitionSpec as P

MESH = pl.DeviceIdType.MESH
BF = jnp.bfloat16
F32 = jnp.float32
LANES = 128
CHUNK = 4


def dot(x, y, dims=((1,), (0,))):
    return lax.dot_general(x, y, (dims, ((), ())), preferred_element_type=F32)


def link_counts(link_owner, link_local, pair_dev, pairs):
    target = (link_owner * pair_dev + link_local).reshape(pair_dev, -1, 1)
    hit = target == jnp.arange(pairs, dtype=jnp.int32)[None, None, :]
    return jnp.sum(hit.astype(F32), axis=1)


def fused_kernel(
    n, cuts, amp, coef, ints, counts, coulomb, energy, out,
    msg_out, msg_in, sum_out, sum_in, shuffle, acc, other_counts, other_acc,
    msg_send, msg_recv, sum_send, sum_recv, aux_send, aux_recv,
):
    g, a = lax.axis_index("pairs"), lax.axis_index("aux")
    other = 1 - a
    pair_dev, width, _ = amp.shape
    pao = coef.shape[1]
    rows = pao // 2
    band = rows // n
    tiles = 2 * band
    own = coulomb.shape[0]
    count_tiles = counts.shape[0]

    def partner(k):
        return lax.rem(g + lax.rem(k + n // 2 - 1, n - 1) + 1, n)

    barrier = pltpu.get_barrier_semaphore()

    def greet(k, _):
        pl.semaphore_signal(barrier, inc=1, device_id=(partner(k), a), device_id_type=MESH)
        return 0

    lax.fori_loop(1, n, greet, 0)
    pl.semaphore_signal(barrier, inc=1, device_id=(g, other), device_id_type=MESH)

    mine = pl.ds(pl.multiple_of(a * rows, rows), rows)

    def backproject(q, _):
        half = dot(coef[q, mine, :], amp[q]).astype(BF)
        m = dot(half, coef[q], ((1,), (1,)))
        for side in range(2):
            start = pl.multiple_of((q * 2 + side) * rows, rows)
            shuffle[pl.ds(start, rows), :] = m[:, side * LANES:(side + 1) * LANES]
        return 0

    lax.fori_loop(0, pair_dev, backproject, 0)

    pl.semaphore_wait(barrier, n)
    swap = pltpu.make_async_remote_copy(
        src_ref=counts, dst_ref=other_counts, send_sem=aux_send.at[0], recv_sem=aux_recv.at[0],
        device_id=(g, other), device_id_type=MESH,
    )
    swap.start()
    swap.wait()
    all_counts = counts[...] + other_counts[...]

    def pack(h):
        for side in range(2):
            for r in range(band):
                tile = shuffle[pl.ds(side * rows + h * band + r, pair_dev, stride=2 * rows), :]
                msg_out[h, side * band + r] = tile.astype(BF)
        msg_out[h, tiles:tiles + count_tiles] = all_counts

    def message(h, slot):
        return pltpu.make_async_remote_copy(
            src_ref=msg_out.at[h], dst_ref=msg_in.at[slot], send_sem=msg_send.at[h],
            recv_sem=msg_recv.at[slot], device_id=(h, a), device_id_type=MESH,
        )

    def sums(h, slot):
        return pltpu.make_async_remote_copy(
            src_ref=sum_out.at[h], dst_ref=sum_in.at[slot], send_sem=sum_send.at[h],
            recv_sem=sum_recv.at[slot], device_id=(h, a), device_id_type=MESH,
        )

    def ship(k, _):
        h = partner(k)
        pack(h)
        message(h, g).start()
        return 0

    lax.fori_loop(1, n, ship, 0)
    pack(g)
    msg_in[g] = msg_out[g]

    acc[...] = jnp.zeros_like(acc)

    def ladder(step, _):
        block = ints[pl.ds(step * CHUNK, CHUNK)]
        stacked = block.reshape(CHUNK * width, width)
        wide = jnp.concatenate([block[j] for j in range(CHUNK)], axis=1)
        for pp in range(pair_dev // 2):
            two = amp[2 * pp:2 * pp + 2].reshape(2 * width, width)
            half = dot(two, stacked, ((1,), (1,))).astype(BF)
            turned = jnp.concatenate(
                [
                    jnp.concatenate(
                        [half[i * width:(i + 1) * width, j * width:(j + 1) * width] for i in range(2)],
                        axis=1,
                    )
                    for j in range(CHUNK)
                ],
                axis=0,
            )
            acc[pp] += dot(wide, turned)
        return 0

    lax.fori_loop(0, cuts[0], ladder, 0)

    def take_message(k, _):
        message(partner(k), partner(k)).wait_recv()
        return 0

    lax.fori_loop(1, n, take_message, 0)

    matrix = jnp.concatenate(
        [msg_in[:, tiles + j].reshape(n * pair_dev, LANES) for j in range(count_tiles)], axis=1
    )
    for t in range(0, tiles, 2):
        both = jnp.concatenate(
            [msg_in[:, t + j].reshape(n * pair_dev, LANES) for j in range(2)], axis=1
        )
        total = dot(matrix, both).astype(BF)
        for j in range(2):
            sum_out[:, t + j] = total[:, j * LANES:(j + 1) * LANES].reshape(n, pair_dev, LANES)

    def ship_sums(k, _):
        sums(partner(k), g).start()
        return 0

    lax.fori_loop(1, n, ship_sums, 0)
    sum_in[g] = sum_out[g]

    lax.fori_loop(cuts[0], cuts[1], ladder, 0)

    def take_sums(k, _):
        sums(partner(k), partner(k)).wait_recv()
        return 0

    lax.fori_loop(1, n, take_sums, 0)

    def spread(h, _):
        for side in range(2):
            start = pl.multiple_of((side * n + h) * band * pair_dev, band * pair_dev)
            part = sum_in[h, side * band:(side + 1) * band]
            shuffle[pl.ds(start, band * pair_dev), :] = part.reshape(band * pair_dev, LANES).astype(F32)
        return 0

    lax.fori_loop(0, n, spread, 0)

    def project(pp, _):
        found = []
        for i in range(2):
            p = 2 * pp + i
            s = jnp.concatenate(
                [
                    shuffle[pl.ds(side * rows * pair_dev + p, rows, stride=pair_dev), :].astype(BF)
                    for side in range(2)
                ],
                axis=1,
            )
            y = dot(s, coef[p]).astype(BF)
            found.append(dot(coef[p, mine, :], y, ((0,), (0,))))
        acc[pp] += jnp.concatenate(found, axis=1)
        return 0

    few = own // 2
    lax.fori_loop(other * few, other * few + few, project, 0)
    trade = pltpu.make_async_remote_copy(
        src_ref=acc.at[pl.ds(other * few, few)], dst_ref=other_acc, send_sem=aux_send.at[1],
        recv_sem=aux_recv.at[1], device_id=(g, other), device_id_type=MESH,
    )
    trade.start()
    lax.fori_loop(a * few, a * few + few, project, 0)
    trade.wait()

    for i in range(own):
        lanes = slice((i % 2) * width, (i % 2 + 1) * width)
        reduced = acc[a * few + i // 2, :, lanes] + other_acc[i // 2, :, lanes]
        residual = coulomb[i].astype(F32) + reduced
        line = jnp.broadcast_to(energy[i:i + 1, :], (width, width))
        out[i] = amp[a * own + i].astype(F32) - residual / (line + line.T)

    def finish(k, _):
        message(partner(k), g).wait_send()
        sums(partner(k), g).wait_send()
        return 0

    lax.fori_loop(1, n, finish, 0)


def fused(amplitudes, pno_coef, ladder_ints, coulomb_ints, pno_energy, link_owner, link_local):
    n = lax.axis_size("pairs")
    pair_dev, width, _ = amplitudes.shape
    pao = pno_coef.shape[1]
    pairs = n * pair_dev
    counts = link_counts(link_owner, link_local, pair_dev, pairs).astype(BF)
    count_tiles = pairs // LANES
    counts = jnp.swapaxes(counts.reshape(pair_dev, count_tiles, LANES), 0, 1)
    band = pao // 2 // n
    tiles = 2 * band
    own = coulomb_ints.shape[0]
    steps = ladder_ints.shape[0] // CHUNK
    return pl.pallas_call(
        functools.partial(fused_kernel, n, (steps // 2, steps)),
        out_shape=jax.ShapeDtypeStruct(coulomb_ints.shape, F32),
        in_specs=[pl.BlockSpec(memory_space=pltpu.VMEM)] * 6,
        out_specs=pl.BlockSpec(memory_space=pltpu.VMEM),
        scratch_shapes=[
            pltpu.VMEM((n, tiles + count_tiles, pair_dev, LANES), BF),
            pltpu.VMEM((n, tiles + count_tiles, pair_dev, LANES), BF),
            pltpu.VMEM((n, tiles, pair_dev, LANES), BF),
            pltpu.VMEM((n, tiles, pair_dev, LANES), BF),
            pltpu.VMEM((pair_dev * pao, LANES), F32),
            pltpu.VMEM((pair_dev // 2, width, 2 * width), F32),
            pltpu.VMEM(counts.shape, BF),
            pltpu.VMEM((own // 2, width, 2 * width), F32),
            pltpu.SemaphoreType.DMA((n,)),
            pltpu.SemaphoreType.DMA((n,)),
            pltpu.SemaphoreType.DMA((n,)),
            pltpu.SemaphoreType.DMA((n,)),
            pltpu.SemaphoreType.DMA((2,)),
            pltpu.SemaphoreType.DMA((2,)),
        ],
        compiler_params=pltpu.CompilerParams(
            collective_id=0, has_side_effects=True, vmem_limit_bytes=48 * 2**20
        ),
    )(amplitudes, pno_coef, ladder_ints, counts, coulomb_ints, pno_energy)


def general(amplitudes, pno_coef, ladder_ints, coulomb_ints, pno_energy, link_owner, link_local):
    groups, parts = lax.axis_size("pairs"), lax.axis_size("aux")
    devices = groups * parts
    pair_dev, width, _ = amplitudes.shape
    pao = pno_coef.shape[1]
    own = coulomb_ints.shape[0]
    first = lax.axis_index("aux") * own
    both = ("pairs", "aux")
    counts = link_counts(link_owner, link_local, pair_dev, groups * pair_dev)
    matrix = lax.all_gather(lax.psum(counts, "aux"), "pairs", axis=0, tiled=True).astype(BF)
    amp = lax.dynamic_slice_in_dim(amplitudes, first, own, 0)
    coef = lax.dynamic_slice_in_dim(pno_coef, first, own, 0)
    half = jnp.einsum("qac,qcd->qad", coef, amp, preferred_element_type=F32).astype(BF)
    back = jnp.einsum("qad,qbd->qab", half, coef, preferred_element_type=F32).astype(BF)
    back = jnp.swapaxes(back.reshape(own, devices, -1), 0, 1)
    back = lax.all_to_all(back, both, split_axis=0, concat_axis=0, tiled=True)
    total = dot(matrix, back.reshape(devices * own, -1)).astype(BF)
    total = lax.all_to_all(
        total.reshape(devices, own, -1), both, split_axis=0, concat_axis=0, tiled=True
    )
    total = jnp.swapaxes(total, 0, 1).reshape(own, pao, pao)
    near = jnp.einsum("pab,pbd->pad", total, coef, preferred_element_type=F32).astype(BF)
    linked = jnp.einsum("pac,pad->pcd", coef, near, preferred_element_type=F32)

    def ladder_terms(amp_p):
        ladder_half = jnp.einsum(
            "qcd,de->qce", ladder_ints, amp_p, preferred_element_type=F32
        ).astype(BF)
        return jnp.einsum("qce,qfe->cf", ladder_half, ladder_ints, preferred_element_type=F32)

    ladder = lax.psum_scatter(
        lax.map(ladder_terms, amplitudes), "aux", scatter_dimension=0, tiled=True
    )
    residual = coulomb_ints.astype(F32) + ladder + linked
    denominator = pno_energy[:, :, None] + pno_energy[:, None, :]
    return amp.astype(F32) - residual / denominator


def local(*arrays):
    amplitudes, pno_coef, ladder_ints = arrays[:3]
    n = lax.axis_size("pairs")
    fits = (
        lax.axis_size("aux") == 2
        and amplitudes.shape[1] == LANES
        and pno_coef.shape[1] == 2 * LANES
        and amplitudes.shape[0] == 16
        and LANES % (8 * n) == 0
        and n * 16 % LANES == 0
        and ladder_ints.shape[0] % CHUNK == 0
    )
    return fused(*arrays) if fits else general(*arrays)


def solution(mesh):
    in_specs = (
        P("pairs", None, None),
        P("pairs", None, None),
        P("aux", None, None),
        P(("pairs", "aux"), None, None),
        P(("pairs", "aux"), None),
        P(("pairs", "aux"), None),
        P(("pairs", "aux"), None),
    )
    out_specs = P(("pairs", "aux"), None, None)
    return jax.shard_map(local, mesh=mesh, in_specs=in_specs, out_specs=out_specs, check_vma=False)
```

time: 597 us -> 109 us (0.18)
  waiting for transfers between devices: 273 us -> 0 us
  matrix products: 134 us -> 0 us
  local copies, waits for them, and re-layouts: 120 us -> 4.86 us
  Pallas kernels: 0 us -> 103 us
  starting transfers between devices: 23.3 us -> 0 us
  other arithmetic: 16.4 us -> 0.78 us
  blocking collectives: 15.4 us -> 0 us
  between operations: 13.5 us -> 0.04 us
    all_to_all x2 -> x0, waiting for transfers between devices: 219 us -> none  [the longest x1 154 us: local(): lax.all_to_all(coef_items, 'pairs', split_axis=0, concat_axis=0, tiled=True)]
    dot_general x48 -> x0, matrix products: 134 us -> none  [the longest x16 122 us: pair_terms(): jnp.einsum('qce,qfe->cf', ladder_half, ladder_ints, preferred_element_typ...]
    gather x34 -> x0, local copies, waits for them, and re-layouts: 119 us -> none  [the longest x16 64.1 us: pair_terms(): coef_q = flat_coef[key_row]]
    pallas_call x0 -> x1, Pallas kernels: none -> 103 us  [fused(): pl.pallas_call(functools.partial(fused_kernel, n, (steps // 2, steps)), o...]
    psum x1 -> x0, waiting for transfers between devices: 53.7 us -> none  [local(): summed = lax.psum(partial_value, 'aux')]
    all_to_all x2 -> x0, starting transfers between devices: 23.3 us -> none  [the longest x1 18.6 us: local(): lax.all_to_all(coef_items, 'pairs', split_axis=0, concat_axis=0, tiled=True)]
    all_to_all x1 -> x0, blocking collectives: 15.4 us -> none  [local(): lax.all_to_all(wanted.reshape(groups, capacity), 'pairs', split_axis=0, c...]
    select_n x18 -> x0, other arithmetic: 11.8 us -> none  [the longest x1 7.22 us: local(): coef_items = jnp.where(present[:, :, None, None], pno_coef[picked], nothing)]
  transfers between devices with their start and end apart: 3 -> 0, of which waited for: 3 -> 0; matrix products, arithmetic and copies ran while one was open for 2% -> 0% of each run, Pallas kernels for 0% -> 0%
where the time goes in v1:
time: 109 us; the launch traced here: 108 us
  Pallas kernels  103 us (94%)
  local copies, waits for them, and re-layouts  4.86 us (4%)
    pallas_call x1, Pallas kernels, fused(): pl.pallas_call(functools.partial(fused_kernel, n, (steps // 2, steps)), o...  103 us
    unnamed x9, local copies, waits for them, and re-layouts  4.69 us

profile of v1, /device:TPU:0, one launch (start us, length us, event | category | flops | bytes accessed | tf_op | source)
XLA Modules:
  0.0 108.5 jit_solution(580216631860141446)
XLA Ops:
  0.0 0.7 add_reduce_fusion
  0.7 0.1 eq.15
  0.8 0.1 copy.9
  0.9 0.1 convert_reduce_fusion
  1.0 0.0 copy-start
  1.0 1.2 %copy-done = bf16[16,256,128]{2,1,0:T(8,128)(2,1)S(1)} copy-done((bf16[16,256,128]{2,1,0:T(8,128)(2,1)S(1)}, bf16[16,256,128]{2,1,0:T(8,128)(2,1)}, u32[]{:S(2)}) %copy-start) | copy-done | bytes 1048600
  2.2 0.0 copy-start.1
  2.2 1.0 copy-done.1
  3.2 0.0 copy-start.2
  3.2 0.9 copy-done.2
  4.2 0.0 copy-start.3
  4.2 0.7 copy-done.3
  4.9 102.8 %shard_map.73 = f32[8,128,128]{2,1,0:T(8,128)S(1)} custom-call(bf16[16,128,128]{2,1,0:T(8,128)(2,1)S(1)} %copy-done.1, bf16[16,256,128]{2,1,0:T(8,128)(2,1)S(1)} %copy-done, bf16[160,128,128]{2,1,0:T(8,128)(2,1)} %ints.1, bf16[2,16,128]{2,1,0:T(8,128)(2,1)S(1)} %bitcast_bitcast_fusion.counts, bf16[8,128,128]{2,1,0:T(8,128)(2,1)S(1)} %copy-done.2, ...), custom_call_target="tpu_custom_call" | custom-call | tf_op jit(solution)/shard_map/pallas_call | solution.py:222
  107.7 0.8 copy.14
  (1 shorter events, 0.0 us)
Async XLA Ops:
  1.0 1.2 %copy-start = (bf16[16,256,128]{2,1,0:T(8,128)(2,1)S(1)}, bf16[16,256,128]{2,1,0:T(8,128)(2,1)}, u32[]{:S(2)}) copy-start(bf16[16,256,128]{2,1,0:T(8,128)(2,1)} %coef.1) | copy-start | bytes 3145732
  2.2 1.0 copy-start.1
  3.2 0.9 copy-start.2
  4.2 0.7 copy-start.3

commit v2 on v1

--- a/solution.py
+++ b/solution.py
@@ -25,9 +25,10 @@
 
 
 def fused_kernel(
-    n, cuts, amp, coef, ints, counts, coulomb, energy, out,
+    n, cuts, amp_hbm, coef_hbm, ints_hbm, counts_hbm, coulomb_hbm, energy_hbm, out,
+    amp, coef, ints, counts, coulomb, energy,
     msg_out, msg_in, sum_out, sum_in, shuffle, acc, other_counts, other_acc,
-    msg_send, msg_recv, sum_send, sum_recv, aux_send, aux_recv,
+    load, msg_send, msg_recv, sum_send, sum_recv, aux_send, aux_recv,
 ):
     g, a = lax.axis_index("pairs"), lax.axis_index("aux")
     other = 1 - a
@@ -35,9 +36,21 @@
     pao = coef.shape[1]
     rows = pao // 2
     band = rows // n
-    tiles = 2 * band
     own = coulomb.shape[0]
     count_tiles = counts.shape[0]
+    spans = ((0, count_tiles + band), (count_tiles + band, band))
+
+    loads = [
+        pltpu.make_async_copy(src, dst, load.at[i])
+        for i, (src, dst) in enumerate(
+            (
+                (amp_hbm, amp), (coef_hbm, coef), (counts_hbm, counts),
+                (ints_hbm, ints), (coulomb_hbm, coulomb), (energy_hbm, energy),
+            )
+        )
+    ]
+    for copy in loads:
+        copy.start()
 
     def partner(k):
         return lax.rem(g + lax.rem(k + n // 2 - 1, n - 1) + 1, n)
@@ -50,6 +63,8 @@
 
     lax.fori_loop(1, n, greet, 0)
     pl.semaphore_signal(barrier, inc=1, device_id=(g, other), device_id_type=MESH)
+    for copy in loads[:3]:
+        copy.wait()
 
     mine = pl.ds(pl.multiple_of(a * rows, rows), rows)
 
@@ -61,55 +76,68 @@
             shuffle[pl.ds(start, rows), :] = m[:, side * LANES:(side + 1) * LANES]
         return 0
 
-    lax.fori_loop(0, pair_dev, backproject, 0)
-
+    lax.fori_loop(0, pair_dev // 2, backproject, 0, unroll=4)
     pl.semaphore_wait(barrier, n)
     swap = pltpu.make_async_remote_copy(
         src_ref=counts, dst_ref=other_counts, send_sem=aux_send.at[0], recv_sem=aux_recv.at[0],
         device_id=(g, other), device_id_type=MESH,
     )
     swap.start()
+    lax.fori_loop(pair_dev // 2, pair_dev, backproject, 0, unroll=4)
     swap.wait()
     all_counts = counts[...] + other_counts[...]
 
-    def pack(h):
-        for side in range(2):
-            for r in range(band):
-                tile = shuffle[pl.ds(side * rows + h * band + r, pair_dev, stride=2 * rows), :]
-                msg_out[h, side * band + r] = tile.astype(BF)
-        msg_out[h, tiles:tiles + count_tiles] = all_counts
-
-    def message(h, slot):
+    def pack(h, side):
+        for r in range(band):
+            tile = shuffle[pl.ds(side * rows + h * band + r, pair_dev, stride=2 * rows), :]
+            msg_out[h, count_tiles + side * band + r] = tile.astype(BF)
+        if side == 0:
+            msg_out[h, :count_tiles] = all_counts
+
+    def message(side, h, slot):
+        part = pl.ds(*spans[side])
         return pltpu.make_async_remote_copy(
-            src_ref=msg_out.at[h], dst_ref=msg_in.at[slot], send_sem=msg_send.at[h],
-            recv_sem=msg_recv.at[slot], device_id=(h, a), device_id_type=MESH,
+            src_ref=msg_out.at[h, part], dst_ref=msg_in.at[slot, part],
+            send_sem=msg_send.at[side, h], recv_sem=msg_recv.at[side, slot],
+            device_id=(h, a), device_id_type=MESH,
         )
 
-    def sums(h, slot):
+    def sums(side, h, slot):
+        part = pl.ds(side * band, band)
         return pltpu.make_async_remote_copy(
-            src_ref=sum_out.at[h], dst_ref=sum_in.at[slot], send_sem=sum_send.at[h],
-            recv_sem=sum_recv.at[slot], device_id=(h, a), device_id_type=MESH,
+            src_ref=sum_out.at[h, part], dst_ref=sum_in.at[slot, part],
+            send_sem=sum_send.at[side, h], recv_sem=sum_recv.at[side, slot],
+            device_id=(h, a), device_id_type=MESH,
         )
 
-    def ship(k, _):
+    def ship(side, k, _):
         h = partner(k)
-        pack(h)
-        message(h, g).start()
+        pack(h, side)
+        message(side, h, g).start()
         return 0
 
-    lax.fori_loop(1, n, ship, 0)
-    pack(g)
+    for side in range(2):
+        lax.fori_loop(1, n, functools.partial(ship, side), 0)
+    for side in range(2):
+        pack(g, side)
     msg_in[g] = msg_out[g]
 
     acc[...] = jnp.zeros_like(acc)
+    for copy in loads[3:]:
+        copy.wait()
 
     def ladder(step, _):
         block = ints[pl.ds(step * CHUNK, CHUNK)]
-        stacked = block.reshape(CHUNK * width, width)
+        flipped = jnp.concatenate([block[j].T for j in range(CHUNK)], axis=1)
         wide = jnp.concatenate([block[j] for j in range(CHUNK)], axis=1)
+
+        def first(pp):
+            two = amp[2 * pp:2 * pp + 2].reshape(2 * width, width)
+            return dot(two, flipped).astype(BF)
+
+        half = first(0)
         for pp in range(pair_dev // 2):
-            two = amp[2 * pp:2 * pp + 2].reshape(2 * width, width)
-            half = dot(two, stacked, ((1,), (1,))).astype(BF)
+            coming = first(pp + 1) if pp + 1 < pair_dev // 2 else None
             turned = jnp.concatenate(
                 [
                     jnp.concatenate(
@@ -121,52 +149,60 @@
                 axis=0,
             )
             acc[pp] += dot(wide, turned)
+            half = coming
         return 0
 
-    lax.fori_loop(0, cuts[0], ladder, 0)
-
-    def take_message(k, _):
-        message(partner(k), partner(k)).wait_recv()
-        return 0
-
-    lax.fori_loop(1, n, take_message, 0)
-
-    matrix = jnp.concatenate(
-        [msg_in[:, tiles + j].reshape(n * pair_dev, LANES) for j in range(count_tiles)], axis=1
-    )
-    for t in range(0, tiles, 2):
-        both = jnp.concatenate(
-            [msg_in[:, t + j].reshape(n * pair_dev, LANES) for j in range(2)], axis=1
+    def take_messages(side):
+        def take(k, _):
+            message(side, partner(k), partner(k)).wait_recv()
+            return 0
+
+        lax.fori_loop(1, n, take, 0)
+
+    def add_up(side):
+        matrix = jnp.concatenate(
+            [msg_in[:, j].reshape(n * pair_dev, LANES) for j in range(count_tiles)], axis=1
         )
-        total = dot(matrix, both).astype(BF)
-        for j in range(2):
-            sum_out[:, t + j] = total[:, j * LANES:(j + 1) * LANES].reshape(n, pair_dev, LANES)
-
-    def ship_sums(k, _):
-        sums(partner(k), g).start()
-        return 0
-
-    lax.fori_loop(1, n, ship_sums, 0)
+        for t in range(side * band, (side + 1) * band, 2):
+            both = jnp.concatenate(
+                [msg_in[:, count_tiles + t + j].reshape(n * pair_dev, LANES) for j in range(2)],
+                axis=1,
+            )
+            total = dot(matrix, both).astype(BF)
+            for j in range(2):
+                sum_out[:, t + j] = total[:, j * LANES:(j + 1) * LANES].reshape(n, pair_dev, LANES)
+
+        def ship_sums(k, _):
+            sums(side, partner(k), g).start()
+            return 0
+
+        lax.fori_loop(1, n, ship_sums, 0)
+
+    start = 0
+    for side in range(2):
+        lax.fori_loop(start, cuts[side], ladder, 0)
+        start = cuts[side]
+        take_messages(side)
+        add_up(side)
     sum_in[g] = sum_out[g]
-
-    lax.fori_loop(cuts[0], cuts[1], ladder, 0)
-
-    def take_sums(k, _):
-        sums(partner(k), partner(k)).wait_recv()
-        return 0
-
-    lax.fori_loop(1, n, take_sums, 0)
-
-    def spread(h, _):
-        for side in range(2):
-            start = pl.multiple_of((side * n + h) * band * pair_dev, band * pair_dev)
+    lax.fori_loop(start, cuts[2], ladder, 0)
+
+    for side in range(2):
+        def take_sums(k, _):
+            sums(side, partner(k), partner(k)).wait_recv()
+            return 0
+
+        lax.fori_loop(1, n, take_sums, 0)
+
+        def spread(h, _):
+            place = pl.multiple_of((side * n + h) * band * pair_dev, band * pair_dev)
             part = sum_in[h, side * band:(side + 1) * band]
-            shuffle[pl.ds(start, band * pair_dev), :] = part.reshape(band * pair_dev, LANES).astype(F32)
-        return 0
-
-    lax.fori_loop(0, n, spread, 0)
-
-    def project(pp, _):
+            shuffle[pl.ds(place, band * pair_dev), :] = part.reshape(band * pair_dev, LANES).astype(F32)
+            return 0
+
+        lax.fori_loop(0, n, spread, 0, unroll=4)
+
+    def project(pp):
         found = []
         for i in range(2):
             p = 2 * pp + i
@@ -180,16 +216,17 @@
             y = dot(s, coef[p]).astype(BF)
             found.append(dot(coef[p, mine, :], y, ((0,), (0,))))
         acc[pp] += jnp.concatenate(found, axis=1)
-        return 0
 
     few = own // 2
-    lax.fori_loop(other * few, other * few + few, project, 0)
+    for j in range(few):
+        project(other * few + j)
     trade = pltpu.make_async_remote_copy(
         src_ref=acc.at[pl.ds(other * few, few)], dst_ref=other_acc, send_sem=aux_send.at[1],
         recv_sem=aux_recv.at[1], device_id=(g, other), device_id_type=MESH,
     )
     trade.start()
-    lax.fori_loop(a * few, a * few + few, project, 0)
+    for j in range(few):
+        project(a * few + j)
     trade.wait()
 
     for i in range(own):
@@ -199,12 +236,13 @@
         line = jnp.broadcast_to(energy[i:i + 1, :], (width, width))
         out[i] = amp[a * own + i].astype(F32) - residual / (line + line.T)
 
-    def finish(k, _):
-        message(partner(k), g).wait_send()
-        sums(partner(k), g).wait_send()
-        return 0
-
-    lax.fori_loop(1, n, finish, 0)
+    for side in range(2):
+        def finish(k, _):
+            message(side, partner(k), g).wait_send()
+            sums(side, partner(k), g).wait_send()
+            return 0
+
+        lax.fori_loop(1, n, finish, 0)
 
 
 def fused(amplitudes, pno_coef, ladder_ints, coulomb_ints, pno_energy, link_owner, link_local):
@@ -219,12 +257,14 @@
     tiles = 2 * band
     own = coulomb_ints.shape[0]
     steps = ladder_ints.shape[0] // CHUNK
+    operands = (amplitudes, pno_coef, ladder_ints, counts, coulomb_ints, pno_energy)
     return pl.pallas_call(
-        functools.partial(fused_kernel, n, (steps // 2, steps)),
+        functools.partial(fused_kernel, n, (steps // 4, steps // 2, steps)),
         out_shape=jax.ShapeDtypeStruct(coulomb_ints.shape, F32),
-        in_specs=[pl.BlockSpec(memory_space=pltpu.VMEM)] * 6,
+        in_specs=[pl.BlockSpec(memory_space=pl.ANY)] * 6,
         out_specs=pl.BlockSpec(memory_space=pltpu.VMEM),
         scratch_shapes=[
+            *(pltpu.VMEM(x.shape, x.dtype) for x in operands),
             pltpu.VMEM((n, tiles + count_tiles, pair_dev, LANES), BF),
             pltpu.VMEM((n, tiles + count_tiles, pair_dev, LANES), BF),
             pltpu.VMEM((n, tiles, pair_dev, LANES), BF),
@@ -233,17 +273,18 @@
             pltpu.VMEM((pair_dev // 2, width, 2 * width), F32),
             pltpu.VMEM(counts.shape, BF),
             pltpu.VMEM((own // 2, width, 2 * width), F32),
-            pltpu.SemaphoreType.DMA((n,)),
-            pltpu.SemaphoreType.DMA((n,)),
-            pltpu.SemaphoreType.DMA((n,)),
-            pltpu.SemaphoreType.DMA((n,)),
+            pltpu.SemaphoreType.DMA((len(operands),)),
+            pltpu.SemaphoreType.DMA((2, n)),
+            pltpu.SemaphoreType.DMA((2, n)),
+            pltpu.SemaphoreType.DMA((2, n)),
+            pltpu.SemaphoreType.DMA((2, n)),
             pltpu.SemaphoreType.DMA((2,)),
             pltpu.SemaphoreType.DMA((2,)),
         ],
         compiler_params=pltpu.CompilerParams(
-            collective_id=0, has_side_effects=True, vmem_limit_bytes=48 * 2**20
+            collective_id=0, has_side_effects=True, vmem_limit_bytes=62 * 2**20
         ),
-    )(amplitudes, pno_coef, ladder_ints, counts, coulomb_ints, pno_energy)
+    )(*operands)
 
 
 def general(amplitudes, pno_coef, ladder_ints, coulomb_ints, pno_energy, link_owner, link_local):

time: 109 us -> 79.5 us (0.73)
  Pallas kernels: 103 us -> 75.9 us
  local copies, waits for them, and re-layouts: 4.86 us -> 2.64 us
    pallas_call x1, Pallas kernels: 103 us -> 75.9 us  [fused(): pl.pallas_call(functools.partial(fused_kernel, n, (steps // 4, steps // 2...]
    unnamed x9 -> x1, local copies, waits for them, and re-layouts: 4.69 us -> 1.87 us
where the time goes in v2:
time: 79.5 us; the launch traced here: 79.3 us
  Pallas kernels  75.9 us (95%)
  local copies, waits for them, and re-layouts  2.64 us (3%)
    pallas_call x1, Pallas kernels, fused(): pl.pallas_call(functools.partial(fused_kernel, n, (steps // 4, steps // 2...  75.9 us
    unnamed x1, local copies, waits for them, and re-layouts  1.87 us

profile of v2, /device:TPU:0, one launch (start us, length us, event | category | flops | bytes accessed | tf_op | source)
XLA Modules:
  0.0 79.3 jit_solution(10648390965629593386)
XLA Ops:
  0.0 0.7 add_reduce_fusion
  0.7 0.1 eq.15
  0.8 0.1 copy.9
  0.9 0.1 convert_reduce_fusion
  1.0 0.6 bitcast_bitcast_fusion.counts_hbm
  1.6 75.9 %shard_map.73 = f32[8,128,128]{2,1,0:T(8,128)} custom-call(bf16[16,128,128]{2,1,0:T(8,128)(2,1)} %amp_hbm.1, bf16[16,256,128]{2,1,0:T(8,128)(2,1)} %coef_hbm.1, bf16[160,128,128]{2,1,0:T(8,128)(2,1)} %ints_hbm.1, bf16[2,16,128]{2,1,0:T(8,128)(2,1)} %bitcast_bitcast_fusion.counts_hbm, bf16[8,128,128]{2,1,0:T(8,128)(2,1)} %coulomb_hbm.1, f32[8,128]{1,0:T(8,128)} %energy_hbm.1), custom_call_target="tpu_custom_call" | custom-call | tf_op jit(solution)/shard_map/pallas_call | solution.py:261
  77.4 1.9 %copy.14 = f32[8,128,128]{2,1,0:T(8,128)} copy(f32[8,128,128]{2,1,0:T(8,128)} %shard_map.73) | data formatting | bytes 1048576

commit v3 on v2

--- a/solution.py
+++ b/solution.py
@@ -25,8 +25,8 @@
 
 
 def fused_kernel(
-    n, cuts, amp_hbm, coef_hbm, ints_hbm, counts_hbm, coulomb_hbm, energy_hbm, out,
-    amp, coef, ints, counts, coulomb, energy,
+    n, cuts, amp_hbm, coef_hbm, ints_hbm, owner_hbm, local_hbm, coulomb_hbm, energy_hbm, out,
+    amp, coef, ints, owner, local_index, coulomb, energy, counts,
     msg_out, msg_in, sum_out, sum_in, shuffle, acc, other_counts, other_acc,
     load, msg_send, msg_recv, sum_send, sum_recv, aux_send, aux_recv,
 ):
@@ -44,7 +44,7 @@
         pltpu.make_async_copy(src, dst, load.at[i])
         for i, (src, dst) in enumerate(
             (
-                (amp_hbm, amp), (coef_hbm, coef), (counts_hbm, counts),
+                (amp_hbm, amp), (coef_hbm, coef), (owner_hbm, owner), (local_hbm, local_index),
                 (ints_hbm, ints), (coulomb_hbm, coulomb), (energy_hbm, energy),
             )
         )
@@ -63,7 +63,7 @@
 
     lax.fori_loop(1, n, greet, 0)
     pl.semaphore_signal(barrier, inc=1, device_id=(g, other), device_id_type=MESH)
-    for copy in loads[:3]:
+    for copy in loads[:4]:
         copy.wait()
 
     mine = pl.ds(pl.multiple_of(a * rows, rows), rows)
@@ -76,6 +76,19 @@
             shuffle[pl.ds(start, rows), :] = m[:, side * LANES:(side + 1) * LANES]
         return 0
 
+    slots = owner.shape[1]
+    per_pair = slots // pair_dev
+    target = owner[...] * pair_dev + local_index[...]
+    hit = lax.broadcasted_iota(jnp.int32, (n * pair_dev, slots), 0) == target
+    first_slot = lax.broadcasted_iota(jnp.int32, (pair_dev, slots), 0) * per_pair
+    slot = lax.broadcasted_iota(jnp.int32, (pair_dev, slots), 1)
+    own_slot = (slot >= first_slot) & (slot < first_slot + per_pair)
+    found = dot(
+        jnp.where(own_slot, 1.0, 0.0).astype(BF), jnp.where(hit, 1.0, 0.0).astype(BF), ((1,), (1,))
+    ).astype(BF)
+    for j in range(count_tiles):
+        counts[j] = found[:, j * LANES:(j + 1) * LANES]
+
     lax.fori_loop(0, pair_dev // 2, backproject, 0, unroll=4)
     pl.semaphore_wait(barrier, n)
     swap = pltpu.make_async_remote_copy(
@@ -123,7 +136,7 @@
     msg_in[g] = msg_out[g]
 
     acc[...] = jnp.zeros_like(acc)
-    for copy in loads[3:]:
+    for copy in loads[4:]:
         copy.wait()
 
     def ladder(step, _):
@@ -131,24 +144,28 @@
         flipped = jnp.concatenate([block[j].T for j in range(CHUNK)], axis=1)
         wide = jnp.concatenate([block[j] for j in range(CHUNK)], axis=1)
 
-        def first(pp):
-            two = amp[2 * pp:2 * pp + 2].reshape(2 * width, width)
-            return dot(two, flipped).astype(BF)
+        def first(quad):
+            four = amp[4 * quad:4 * quad + 4].reshape(4 * width, width)
+            return dot(four, flipped).astype(BF)
 
         half = first(0)
-        for pp in range(pair_dev // 2):
-            coming = first(pp + 1) if pp + 1 < pair_dev // 2 else None
-            turned = jnp.concatenate(
-                [
-                    jnp.concatenate(
-                        [half[i * width:(i + 1) * width, j * width:(j + 1) * width] for i in range(2)],
-                        axis=1,
-                    )
-                    for j in range(CHUNK)
-                ],
-                axis=0,
-            )
-            acc[pp] += dot(wide, turned)
+        for quad in range(pair_dev // 4):
+            coming = first(quad + 1) if quad + 1 < pair_dev // 4 else None
+            for pp in range(2):
+                turned = jnp.concatenate(
+                    [
+                        jnp.concatenate(
+                            [
+                                half[i * width:(i + 1) * width, j * width:(j + 1) * width]
+                                for i in (2 * pp, 2 * pp + 1)
+                            ],
+                            axis=1,
+                        )
+                        for j in range(CHUNK)
+                    ],
+                    axis=0,
+                )
+                acc[2 * quad + pp] += dot(wide, turned)
             half = coming
         return 0
 
@@ -185,9 +202,8 @@
         take_messages(side)
         add_up(side)
     sum_in[g] = sum_out[g]
-    lax.fori_loop(start, cuts[2], ladder, 0)
-
-    for side in range(2):
+
+    def receive_sums(side):
         def take_sums(k, _):
             sums(side, partner(k), partner(k)).wait_recv()
             return 0
@@ -202,31 +218,32 @@
 
         lax.fori_loop(0, n, spread, 0, unroll=4)
 
-    def project(pp):
+    def project(side, pp):
         found = []
         for i in range(2):
             p = 2 * pp + i
-            s = jnp.concatenate(
-                [
-                    shuffle[pl.ds(side * rows * pair_dev + p, rows, stride=pair_dev), :].astype(BF)
-                    for side in range(2)
-                ],
-                axis=1,
-            )
-            y = dot(s, coef[p]).astype(BF)
+            s = shuffle[pl.ds(side * rows * pair_dev + p, rows, stride=pair_dev), :].astype(BF)
+            y = dot(s, coef[p, side * LANES:(side + 1) * LANES, :]).astype(BF)
             found.append(dot(coef[p, mine, :], y, ((0,), (0,))))
         acc[pp] += jnp.concatenate(found, axis=1)
 
+    lax.fori_loop(start, cuts[2], ladder, 0)
+    receive_sums(0)
+    for pp in range(pair_dev // 2):
+        project(0, pp)
+    lax.fori_loop(cuts[2], cuts[3], ladder, 0)
+    receive_sums(1)
+
     few = own // 2
     for j in range(few):
-        project(other * few + j)
+        project(1, other * few + j)
     trade = pltpu.make_async_remote_copy(
         src_ref=acc.at[pl.ds(other * few, few)], dst_ref=other_acc, send_sem=aux_send.at[1],
         recv_sem=aux_recv.at[1], device_id=(g, other), device_id_type=MESH,
     )
     trade.start()
     for j in range(few):
-        project(a * few + j)
+        project(1, a * few + j)
     trade.wait()
 
     for i in range(own):
@@ -250,28 +267,30 @@
     pair_dev, width, _ = amplitudes.shape
     pao = pno_coef.shape[1]
     pairs = n * pair_dev
-    counts = link_counts(link_owner, link_local, pair_dev, pairs).astype(BF)
     count_tiles = pairs // LANES
-    counts = jnp.swapaxes(counts.reshape(pair_dev, count_tiles, LANES), 0, 1)
     band = pao // 2 // n
     tiles = 2 * band
     own = coulomb_ints.shape[0]
     steps = ladder_ints.shape[0] // CHUNK
-    operands = (amplitudes, pno_coef, ladder_ints, counts, coulomb_ints, pno_energy)
+    operands = (
+        amplitudes, pno_coef, ladder_ints, link_owner.reshape(1, -1), link_local.reshape(1, -1),
+        coulomb_ints, pno_energy,
+    )
     return pl.pallas_call(
-        functools.partial(fused_kernel, n, (steps // 4, steps // 2, steps)),
+        functools.partial(fused_kernel, n, (steps // 4, steps // 2, 17 * steps // 20, steps)),
         out_shape=jax.ShapeDtypeStruct(coulomb_ints.shape, F32),
-        in_specs=[pl.BlockSpec(memory_space=pl.ANY)] * 6,
+        in_specs=[pl.BlockSpec(memory_space=pl.ANY)] * len(operands),
         out_specs=pl.BlockSpec(memory_space=pltpu.VMEM),
         scratch_shapes=[
             *(pltpu.VMEM(x.shape, x.dtype) for x in operands),
+            pltpu.VMEM((count_tiles, pair_dev, LANES), BF),
             pltpu.VMEM((n, tiles + count_tiles, pair_dev, LANES), BF),
             pltpu.VMEM((n, tiles + count_tiles, pair_dev, LANES), BF),
             pltpu.VMEM((n, tiles, pair_dev, LANES), BF),
             pltpu.VMEM((n, tiles, pair_dev, LANES), BF),
             pltpu.VMEM((pair_dev * pao, LANES), F32),
             pltpu.VMEM((pair_dev // 2, width, 2 * width), F32),
-            pltpu.VMEM(counts.shape, BF),
+            pltpu.VMEM((count_tiles, pair_dev, LANES), BF),
             pltpu.VMEM((own // 2, width, 2 * width), F32),
             pltpu.SemaphoreType.DMA((len(operands),)),
             pltpu.SemaphoreType.DMA((2, n)),
@@ -282,7 +301,7 @@
             pltpu.SemaphoreType.DMA((2,)),
         ],
         compiler_params=pltpu.CompilerParams(
-            collective_id=0, has_side_effects=True, vmem_limit_bytes=62 * 2**20
+            collective_id=0, has_side_effects=True, vmem_limit_bytes=60 * 2**20
         ),
     )(*operands)
 

time: 79.5 us -> 72.8 us (0.916)
  the two profiles are of different devices: /device:TPU:0 before, /device:TPU:27 now
where the time goes in v3:
time: 72.8 us; the launch traced here: 72.6 us
  Pallas kernels  70.8 us (97%)
  local copies, waits for them, and re-layouts  1.87 us (3%)
    pallas_call x1, Pallas kernels, fused(): pl.pallas_call(functools.partial(fused_kernel, n, (steps // 4, steps // 2...  70.8 us
    unnamed x1, local copies, waits for them, and re-layouts  1.87 us

profile of v3, /device:TPU:27, one launch (start us, length us, event | category | flops | bytes accessed | tf_op | source)
XLA Modules:
  0.0 72.6 jit_solution(1836604196729229396)
XLA Ops:
  0.0 70.8 %shard_map.73 = f32[8,128,128]{2,1,0:T(8,128)} custom-call(bf16[16,128,128]{2,1,0:T(8,128)(2,1)} %amp_hbm.1, bf16[16,256,128]{2,1,0:T(8,128)(2,1)} %coef_hbm.1, bf16[160,128,128]{2,1,0:T(8,128)(2,1)} %ints_hbm.1, s32[1,96]{1,0:T(1,128)} %bitcast.2, s32[1,96]{1,0:T(1,128)} %bitcast.3, bf16[8,128,128]{2,1,0:T(8,128)(2,1)} %coulomb_hbm.1, f32[8,128]{1,0:T(8,128)} %energy_hbm.1), custom_call_target="tpu_custom_call" | custom-call | tf_op jit(solution)/shard_map/pallas_call | solution.py:279
  70.8 1.9 %copy.9 = f32[8,128,128]{2,1,0:T(8,128)} copy(f32[8,128,128]{2,1,0:T(8,128)} %shard_map.73) | data formatting | bytes 1048576

commit v4 on v3

--- a/solution.py
+++ b/solution.py
@@ -11,7 +11,8 @@
 BF = jnp.bfloat16
 F32 = jnp.float32
 LANES = 128
-CHUNK = 4
+CHUNK = 8
+BLOCK = 8
 
 
 def dot(x, y, dims=((1,), (0,))):
@@ -27,7 +28,7 @@
 def fused_kernel(
     n, cuts, amp_hbm, coef_hbm, ints_hbm, owner_hbm, local_hbm, coulomb_hbm, energy_hbm, out,
     amp, coef, ints, owner, local_index, coulomb, energy, counts,
-    msg_out, msg_in, sum_out, sum_in, shuffle, acc, other_counts, other_acc,
+    msg_out, msg_in, sum_out, sum_in, shuffle, halves, acc, other_counts, other_acc,
     load, msg_send, msg_recv, sum_send, sum_recv, aux_send, aux_recv,
 ):
     g, a = lax.axis_index("pairs"), lax.axis_index("aux")
@@ -141,32 +142,18 @@
 
     def ladder(step, _):
         block = ints[pl.ds(step * CHUNK, CHUNK)]
-        flipped = jnp.concatenate([block[j].T for j in range(CHUNK)], axis=1)
-        wide = jnp.concatenate([block[j] for j in range(CHUNK)], axis=1)
-
-        def first(quad):
-            four = amp[4 * quad:4 * quad + 4].reshape(4 * width, width)
-            return dot(four, flipped).astype(BF)
-
-        half = first(0)
-        for quad in range(pair_dev // 4):
-            coming = first(quad + 1) if quad + 1 < pair_dev // 4 else None
-            for pp in range(2):
-                turned = jnp.concatenate(
-                    [
-                        jnp.concatenate(
-                            [
-                                half[i * width:(i + 1) * width, j * width:(j + 1) * width]
-                                for i in (2 * pp, 2 * pp + 1)
-                            ],
-                            axis=1,
+        stacked = block.reshape(CHUNK * width, width)
+        flipped = jnp.concatenate([block[j].T for j in range(CHUNK)], axis=0)
+        for b in range(pair_dev // BLOCK):
+            for p in range(0, BLOCK, 2):
+                two = jnp.concatenate([amp[b * BLOCK + p], amp[b * BLOCK + p + 1]], axis=1)
+                half = dot(stacked, two).astype(BF)
+                for i in range(2):
+                    for j in range(CHUNK):
+                        halves[b, (p + i) * width:(p + i + 1) * width, j * width:(j + 1) * width] = (
+                            half[j * width:(j + 1) * width, i * width:(i + 1) * width]
                         )
-                        for j in range(CHUNK)
-                    ],
-                    axis=0,
-                )
-                acc[2 * quad + pp] += dot(wide, turned)
-            half = coming
+            acc[b * BLOCK:(b + 1) * BLOCK] += dot(halves[b], flipped).reshape(BLOCK, width, width)
         return 0
 
     def take_messages(side):
@@ -218,38 +205,31 @@
 
         lax.fori_loop(0, n, spread, 0, unroll=4)
 
-    def project(side, pp):
-        found = []
-        for i in range(2):
-            p = 2 * pp + i
-            s = shuffle[pl.ds(side * rows * pair_dev + p, rows, stride=pair_dev), :].astype(BF)
-            y = dot(s, coef[p, side * LANES:(side + 1) * LANES, :]).astype(BF)
-            found.append(dot(coef[p, mine, :], y, ((0,), (0,))))
-        acc[pp] += jnp.concatenate(found, axis=1)
+    def project(side, p):
+        s = shuffle[pl.ds(side * rows * pair_dev + p, rows, stride=pair_dev), :].astype(BF)
+        y = dot(s, coef[p, side * LANES:(side + 1) * LANES, :]).astype(BF)
+        acc[p] += dot(coef[p, mine, :], y, ((0,), (0,)))
 
     lax.fori_loop(start, cuts[2], ladder, 0)
     receive_sums(0)
-    for pp in range(pair_dev // 2):
-        project(0, pp)
+    for p in range(pair_dev):
+        project(0, p)
     lax.fori_loop(cuts[2], cuts[3], ladder, 0)
     receive_sums(1)
 
-    few = own // 2
-    for j in range(few):
-        project(1, other * few + j)
+    for j in range(own):
+        project(1, other * own + j)
     trade = pltpu.make_async_remote_copy(
-        src_ref=acc.at[pl.ds(other * few, few)], dst_ref=other_acc, send_sem=aux_send.at[1],
+        src_ref=acc.at[pl.ds(other * own, own)], dst_ref=other_acc, send_sem=aux_send.at[1],
         recv_sem=aux_recv.at[1], device_id=(g, other), device_id_type=MESH,
     )
     trade.start()
-    for j in range(few):
-        project(1, a * few + j)
+    for j in range(own):
+        project(1, a * own + j)
     trade.wait()
 
     for i in range(own):
-        lanes = slice((i % 2) * width, (i % 2 + 1) * width)
-        reduced = acc[a * few + i // 2, :, lanes] + other_acc[i // 2, :, lanes]
-        residual = coulomb[i].astype(F32) + reduced
+        residual = coulomb[i].astype(F32) + (acc[a * own + i] + other_acc[i])
         line = jnp.broadcast_to(energy[i:i + 1, :], (width, width))
         out[i] = amp[a * own + i].astype(F32) - residual / (line + line.T)
 
@@ -289,9 +269,10 @@
             pltpu.VMEM((n, tiles, pair_dev, LANES), BF),
             pltpu.VMEM((n, tiles, pair_dev, LANES), BF),
             pltpu.VMEM((pair_dev * pao, LANES), F32),
-            pltpu.VMEM((pair_dev // 2, width, 2 * width), F32),
+            pltpu.VMEM((pair_dev // BLOCK, BLOCK * width, CHUNK * width), BF),
+            pltpu.VMEM((pair_dev, width, width), F32),
             pltpu.VMEM((count_tiles, pair_dev, LANES), BF),
-            pltpu.VMEM((own // 2, width, 2 * width), F32),
+            pltpu.VMEM((own, width, width), F32),
             pltpu.SemaphoreType.DMA((len(operands),)),
             pltpu.SemaphoreType.DMA((2, n)),
             pltpu.SemaphoreType.DMA((2, n)),

time: 72.8 us -> 79.6 us (1.093)
  the two profiles are of different devices: /device:TPU:27 before, /device:TPU:0 now
where the time goes in v4:
time: 79.6 us; the launch traced here: 78.1 us
  Pallas kernels  76.2 us (96%)
  local copies, waits for them, and re-layouts  1.87 us (2%)
    pallas_call x1, Pallas kernels, fused(): pl.pallas_call(functools.partial(fused_kernel, n, (steps // 4, steps // 2...  76.2 us
    unnamed x1, local copies, waits for them, and re-layouts  1.87 us

profile of v4, /device:TPU:0, one launch (start us, length us, event | category | flops | bytes accessed | tf_op | source)
XLA Modules:
  0.0 78.1 jit_solution(5343235828170298222)
XLA Ops:
  0.0 76.2 %shard_map.73 = f32[8,128,128]{2,1,0:T(8,128)} custom-call(bf16[16,128,128]{2,1,0:T(8,128)(2,1)} %amp_hbm.1, bf16[16,256,128]{2,1,0:T(8,128)(2,1)} %coef_hbm.1, bf16[160,128,128]{2,1,0:T(8,128)(2,1)} %ints_hbm.1, s32[1,96]{1,0:T(1,128)} %bitcast.2, s32[1,96]{1,0:T(1,128)} %bitcast.3, bf16[8,128,128]{2,1,0:T(8,128)(2,1)} %coulomb_hbm.1, f32[8,128]{1,0:T(8,128)} %energy_hbm.1), custom_call_target="tpu_custom_call" | custom-call | tf_op jit(solution)/shard_map/pallas_call | solution.py:259
  76.2 1.9 %copy.9 = f32[8,128,128]{2,1,0:T(8,128)} copy(f32[8,128,128]{2,1,0:T(8,128)} %shard_map.73) | data formatting | bytes 1048576

commit v5 on v3

--- a/solution.py
+++ b/solution.py
@@ -12,6 +12,7 @@
 F32 = jnp.float32
 LANES = 128
 CHUNK = 4
+BLOCK = 8
 
 
 def dot(x, y, dims=((1,), (0,))):
@@ -90,68 +91,19 @@
         counts[j] = found[:, j * LANES:(j + 1) * LANES]
 
     lax.fori_loop(0, pair_dev // 2, backproject, 0, unroll=4)
-    pl.semaphore_wait(barrier, n)
-    swap = pltpu.make_async_remote_copy(
-        src_ref=counts, dst_ref=other_counts, send_sem=aux_send.at[0], recv_sem=aux_recv.at[0],
-        device_id=(g, other), device_id_type=MESH,
-    )
-    swap.start()
-    lax.fori_loop(pair_dev // 2, pair_dev, backproject, 0, unroll=4)
-    swap.wait()
-    all_counts = counts[...] + other_counts[...]
-
-    def pack(h, side):
-        for r in range(band):
-            tile = shuffle[pl.ds(side * rows + h * band + r, pair_dev, stride=2 * rows), :]
-            msg_out[h, count_tiles + side * band + r] = tile.astype(BF)
-        if side == 0:
-            msg_out[h, :count_tiles] = all_counts
-
-    def message(side, h, slot):
-        part = pl.ds(*spans[side])
-        return pltpu.make_async_remote_copy(
-            src_ref=msg_out.at[h, part], dst_ref=msg_in.at[slot, part],
-            send_sem=msg_send.at[side, h], recv_sem=msg_recv.at[side, slot],
-            device_id=(h, a), device_id_type=MESH,
-        )
-
-    def sums(side, h, slot):
-        part = pl.ds(side * band, band)
-        return pltpu.make_async_remote_copy(
-            src_ref=sum_out.at[h, part], dst_ref=sum_in.at[slot, part],
-            send_sem=sum_send.at[side, h], recv_sem=sum_recv.at[side, slot],
-            device_id=(h, a), device_id_type=MESH,
-        )
-
-    def ship(side, k, _):
-        h = partner(k)
-        pack(h, side)
-        message(side, h, g).start()
-        return 0
-
-    for side in range(2):
-        lax.fori_loop(1, n, functools.partial(ship, side), 0)
-    for side in range(2):
-        pack(g, side)
-    msg_in[g] = msg_out[g]
-
-    acc[...] = jnp.zeros_like(acc)
-    for copy in loads[4:]:
-        copy.wait()
-
     def ladder(step, _):
         block = ints[pl.ds(step * CHUNK, CHUNK)]
         flipped = jnp.concatenate([block[j].T for j in range(CHUNK)], axis=1)
         wide = jnp.concatenate([block[j] for j in range(CHUNK)], axis=1)
 
-        def first(quad):
-            four = amp[4 * quad:4 * quad + 4].reshape(4 * width, width)
-            return dot(four, flipped).astype(BF)
+        def first(b):
+            group = amp[BLOCK * b:BLOCK * (b + 1)].reshape(BLOCK * width, width)
+            return dot(group, flipped).astype(BF)
 
         half = first(0)
-        for quad in range(pair_dev // 4):
-            coming = first(quad + 1) if quad + 1 < pair_dev // 4 else None
-            for pp in range(2):
+        for b in range(pair_dev // BLOCK):
+            coming = first(b + 1) if b + 1 < pair_dev // BLOCK else None
+            for pp in range(BLOCK // 2):
                 turned = jnp.concatenate(
                     [
                         jnp.concatenate(
@@ -165,9 +117,58 @@
                     ],
                     axis=0,
                 )
-                acc[2 * quad + pp] += dot(wide, turned)
+                acc[BLOCK // 2 * b + pp] += dot(wide, turned)
             half = coming
         return 0
+
+    acc[...] = jnp.zeros_like(acc)
+    for copy in loads[4:]:
+        copy.wait()
+    lax.fori_loop(0, cuts[0], ladder, 0)
+    pl.semaphore_wait(barrier, n)
+    swap = pltpu.make_async_remote_copy(
+        src_ref=counts, dst_ref=other_counts, send_sem=aux_send.at[0], recv_sem=aux_recv.at[0],
+        device_id=(g, other), device_id_type=MESH,
+    )
+    swap.start()
+    lax.fori_loop(pair_dev // 2, pair_dev, backproject, 0, unroll=4)
+    swap.wait()
+    all_counts = counts[...] + other_counts[...]
+
+    def pack(h, side):
+        for r in range(band):
+            tile = shuffle[pl.ds(side * rows + h * band + r, pair_dev, stride=2 * rows), :]
+            msg_out[h, count_tiles + side * band + r] = tile.astype(BF)
+        if side == 0:
+            msg_out[h, :count_tiles] = all_counts
+
+    def message(side, h, slot):
+        part = pl.ds(*spans[side])
+        return pltpu.make_async_remote_copy(
+            src_ref=msg_out.at[h, part], dst_ref=msg_in.at[slot, part],
+            send_sem=msg_send.at[side, h], recv_sem=msg_recv.at[side, slot],
+            device_id=(h, a), device_id_type=MESH,
+        )
+
+    def sums(side, h, slot):
+        part = pl.ds(side * band, band)
+        return pltpu.make_async_remote_copy(
+            src_ref=sum_out.at[h, part], dst_ref=sum_in.at[slot, part],
+            send_sem=sum_send.at[side, h], recv_sem=sum_recv.at[side, slot],
+            device_id=(h, a), device_id_type=MESH,
+        )
+
+    def ship(side, k, _):
+        h = partner(k)
+        pack(h, side)
+        message(side, h, g).start()
+        return 0
+
+    for side in range(2):
+        lax.fori_loop(1, n, functools.partial(ship, side), 0)
+    for side in range(2):
+        pack(g, side)
+    msg_in[g] = msg_out[g]
 
     def take_messages(side):
         def take(k, _):
@@ -195,10 +196,8 @@
 
         lax.fori_loop(1, n, ship_sums, 0)
 
-    start = 0
     for side in range(2):
-        lax.fori_loop(start, cuts[side], ladder, 0)
-        start = cuts[side]
+        lax.fori_loop(cuts[side], cuts[side + 1], ladder, 0)
         take_messages(side)
         add_up(side)
     sum_in[g] = sum_out[g]
@@ -227,11 +226,11 @@
             found.append(dot(coef[p, mine, :], y, ((0,), (0,))))
         acc[pp] += jnp.concatenate(found, axis=1)
 
-    lax.fori_loop(start, cuts[2], ladder, 0)
+    lax.fori_loop(cuts[2], cuts[3], ladder, 0)
     receive_sums(0)
     for pp in range(pair_dev // 2):
         project(0, pp)
-    lax.fori_loop(cuts[2], cuts[3], ladder, 0)
+    lax.fori_loop(cuts[3], cuts[4], ladder, 0)
     receive_sums(1)
 
     few = own // 2
@@ -277,7 +276,7 @@
         coulomb_ints, pno_energy,
     )
     return pl.pallas_call(
-        functools.partial(fused_kernel, n, (steps // 4, steps // 2, 17 * steps // 20, steps)),
+        functools.partial(fused_kernel, n, (steps // 10, 11 * steps // 40, steps // 2, 17 * steps // 20, steps)),
         out_shape=jax.ShapeDtypeStruct(coulomb_ints.shape, F32),
         in_specs=[pl.BlockSpec(memory_space=pl.ANY)] * len(operands),
         out_specs=pl.BlockSpec(memory_space=pltpu.VMEM),

time: 72.8 us -> 76.6 us (1.052)
  the two profiles are of different devices: /device:TPU:27 before, /device:TPU:0 now
where the time goes in v5:
time: 76.6 us; the launch traced here: 76.1 us
  Pallas kernels  74.2 us (97%)
  local copies, waits for them, and re-layouts  1.87 us (2%)
    pallas_call x1, Pallas kernels, fused(): pl.pallas_call(functools.partial(fused_kernel, n, (steps // 10, 11 * step...  74.2 us
    unnamed x1, local copies, waits for them, and re-layouts  1.87 us

profile of v5, /device:TPU:0, one launch (start us, length us, event | category | flops | bytes accessed | tf_op | source)
XLA Modules:
  0.0 76.1 jit_solution(12600437562128434400)
XLA Ops:
  0.0 74.2 %shard_map.73 = f32[8,128,128]{2,1,0:T(8,128)} custom-call(bf16[16,128,128]{2,1,0:T(8,128)(2,1)} %amp_hbm.1, bf16[16,256,128]{2,1,0:T(8,128)(2,1)} %coef_hbm.1, bf16[160,128,128]{2,1,0:T(8,128)(2,1)} %ints_hbm.1, s32[1,96]{1,0:T(1,128)} %bitcast.2, s32[1,96]{1,0:T(1,128)} %bitcast.3, bf16[8,128,128]{2,1,0:T(8,128)(2,1)} %coulomb_hbm.1, f32[8,128]{1,0:T(8,128)} %energy_hbm.1), custom_call_target="tpu_custom_call" | custom-call | tf_op jit(solution)/shard_map/pallas_call | solution.py:278
  74.2 1.9 %copy.9 = f32[8,128,128]{2,1,0:T(8,128)} copy(f32[8,128,128]{2,1,0:T(8,128)} %shard_map.73) | data formatting | bytes 1048576
